TPU v7x, 512 devices: a whole 4x4x16 slice. The times are simulated.
512 devices in a mesh: row: 32 (over z_hi, x, core), col: 16 (over z_lo, y).
Axes of the slice: x: 4, y: 4, z: 16 (z_hi: 4, z_lo: 4; z = z_hi * 4 + z_lo), core: 2. Of those that a mesh axis runs over, the one named last changes fastest.
Arguments:
- features: bfloat16 [65536, 256], P(('col', 'row')), may hold values from -6 to 6
- weight: bfloat16 [256, 256], replicated, may hold values from -0.375 to 0.375
- grad_out: bfloat16 [65536, 256], P(('row', 'col')), may hold values from -6 to 6
- tiles: bfloat16 [32, 16, 128, 128, 128], P('row', 'col'), may hold values from -0.046875 to 0.046875
- tile_rows: int32 [32, 16, 128], P('row', 'col'), may hold values from 0 to 15, as said below
- tile_cols: int32 [32, 16, 128], P('row', 'col'), may hold values from 0 to 31, as said below
- tile_count: int32 [32, 16], P('row', 'col'), may hold values from 32 to 128, as said below
Outputs:
- hidden: bfloat16 [65536, 256], P(('row', 'col'))
- grad_features: bfloat16 [65536, 256], P(('col', 'row'))
- grad_weight: float32 [256, 256], replicated
Inputs may be any that keep to these rules, and one draw needn't show every extreme that they name: `tile_rows`: within one block the live and unused slots all name distinct tile places. `tile_cols`: paired with tile_rows slot by slot. `tile_count`: some block is full in every draw.
All inputs are finite; a program needn't handle non-finite values.
Results may differ from a plain program's by a relative error of at most 0.03.
Values may be sent and summed in bfloat16 or wider, within the bound.
A program may use at most 64 MiB of HBM per device.

v0:
```python
import jax
import jax.numpy as jnp
from jax import lax
from jax.sharding import PartitionSpec as P

root_half = 0.7071067811865476
inv_root_tau = 0.3989422804014327


def activate(preact):
    return 0.5 * preact * (1.0 + lax.erf(preact * root_half))


def activate_grad(preact):
    return (
        0.5 * (1.0 + lax.erf(preact * root_half))
        + preact * jnp.exp(-0.5 * preact * preact) * inv_root_tau
    )


def spread(tiles_here, out_index, in_index, live_count, source, targets, flip):
    slots = tiles_here.shape[0]
    per_step = min(32, slots)
    steps = slots // per_step
    side = tiles_here.shape[1]
    width = source.shape[2]
    is_live = jnp.arange(slots, dtype=jnp.int32) < live_count
    target_ids = jnp.arange(targets, dtype=jnp.int32)
    form = "tji,tjf->tif" if flip else "tij,tjf->tif"

    def advance(totals, pieces):
        tile_block, out_block, in_block, live_block = pieces
        picked = source[in_block]
        prods = jnp.einsum(form, tile_block, picked, preferred_element_type=jnp.float32)
        select = ((out_block[None, :] == target_ids[:, None]) & live_block[None, :]).astype(
            jnp.bfloat16
        )
        high = prods.astype(jnp.bfloat16)
        low = (prods - high.astype(jnp.float32)).astype(jnp.bfloat16)
        totals = totals + jnp.einsum(
            "st,tif->sif", select, high, preferred_element_type=jnp.float32
        )
        totals = totals + jnp.einsum("st,tif->sif", select, low, preferred_element_type=jnp.float32)
        return (totals, None)

    start = jnp.zeros((targets, side, width), jnp.float32)
    inputs = (
        tiles_here.reshape(steps, per_step, side, side),
        out_index.reshape(steps, per_step),
        in_index.reshape(steps, per_step),
        is_live.reshape(steps, per_step),
    )
    totals, unused = lax.scan(advance, start, inputs)
    return totals.reshape(targets * side, width)


def body(features, weight, grad_out, tiles, tile_rows, tile_cols, tile_count):
    tiles_here = tiles[0, 0]
    rows_here = tile_rows[0, 0]
    cols_here = tile_cols[0, 0]
    live_count = tile_count[0, 0]
    side = tiles_here.shape[1]
    width = features.shape[1]
    own_rows = grad_out.shape[0]
    whole_x = lax.all_gather(features, "row", axis=0, tiled=True)
    col_tiles = whole_x.shape[0] // side
    row_tiles = own_rows * lax.axis_size("col") // side
    partial_value = spread(
        tiles_here,
        rows_here,
        cols_here,
        live_count,
        whole_x.reshape(col_tiles, side, width),
        row_tiles,
        False,
    )
    aggregate = lax.psum_scatter(
        partial_value.astype(jnp.bfloat16), "col", scatter_dimension=0, tiled=True
    )
    preact = jnp.dot(aggregate, weight, preferred_element_type=jnp.float32)
    hidden = activate(preact).astype(jnp.bfloat16)
    pre_grad = (grad_out.astype(jnp.float32) * activate_grad(preact)).astype(jnp.bfloat16)
    weight_term = lax.dot_general(
        aggregate, pre_grad, (((0,), (0,)), ((), ())), preferred_element_type=jnp.float32
    )
    own_prop = lax.dot_general(
        pre_grad, weight, (((1,), (1,)), ((), ())), preferred_element_type=jnp.float32
    ).astype(jnp.bfloat16)
    prop_grad = lax.all_gather(own_prop, "col", axis=0, tiled=True)
    grad_weight = lax.psum(weight_term, ("row", "col"))
    back_terms = spread(
        tiles_here,
        cols_here,
        rows_here,
        live_count,
        prop_grad.reshape(row_tiles, side, width),
        col_tiles,
        True,
    )
    grad_features = lax.psum_scatter(
        back_terms.astype(jnp.bfloat16), "row", scatter_dimension=0, tiled=True
    )
    return (hidden, grad_features, grad_weight)


def solution(mesh):
    return jax.shard_map(
        body,
        mesh=mesh,
        in_specs=(
            P(("col", "row"), None),
            P(),
            P(("row", "col"), None),
            P("row", "col", None, None, None),
            P("row", "col", None),
            P("row", "col", None),
            P("row", "col"),
        ),
        out_specs=(P(("row", "col"), None), P(("col", "row"), None), P()),
        check_vma=False,
    )
```

profile of v0, /device:TPU:1, one launch (start us, length us, event | category | flops | bytes accessed | tf_op | source)
XLA Modules:
  0.0 907.7 jit_solution(10323386538158499618)
XLA Ops:
  12.0 83.2 %all-gather.3.cloned.1.call-done = bf16[4096,256]{1,0:T(8,128)(2,1)} async-done(((bf16[128,256]{1,0:T(8,128)(2,1)}), bf16[4096,256]{1,0:T(8,128)(2,1)}) %all-gather.3.cloned.1.call-update) | async-done | bytes 2097168 | tf_op jit(solution)/shard_map/all_gather | solution.py:65
  95.2 46.4 %while.22 = (s32[]{:T(128)}, f32[16,128,256]{2,0,1:T(8,128)}, s32[4,32]{1,0:T(4,128)S(1)}, pred[4,32]{1,0:T(4,128)(4,1)S(1)}, bf16[4,32,128,128]{3,2,1,0:T(8,128...) while((s32[]{:T(128)}, f32[16,128,256]{2,0,1:T(8,128)}, ...), condition=%wide.region_1.2_spmd.clone, body=%wide.region_0.1_spmd.clone.sunk | while | flops 341314656 | bytes 24122624 | solution.py:53
  97.5 3.2 subtract_convert_fusion.4
  102.0 4.3 fusion.86
  108.6 3.3 subtract_convert_fusion.4
  113.1 4.9 fusion.86
  120.3 3.2 subtract_convert_fusion.4
  124.9 4.9 fusion.86
  129.8 2.3 gather_fusion
  132.1 3.2 subtract_convert_fusion.4
  136.6 4.9 fusion.86
  141.5 3.7 copy.37
  145.3 74.1 %reduce-scatter.3.cloned.1.call-done = bf16[128,256]{1,0:T(8,128)(2,1)} async-done(((bf16[2048,256]{1,0:T(8,128)(2,1)}), bf16[128,256]{1,0:T(8,128)(2,1)}) %reduce-scatter.3.cloned.1.call-update) | async-done | bytes 65552 | tf_op jit(solution)/shard_map/reduce_scatter | solution.py:77
  222.0 6.4 copy.21
  229.4 76.5 %all-gather.5.cloned.1.call-done = bf16[2048,256]{1,0:T(8,128)(2,1)} async-done(((bf16[128,256]{1,0:T(8,128)(2,1)}), bf16[2048,256]{1,0:T(8,128)(2,1)}) %all-gather.5.cloned.1.call-update) | async-done | bytes 1048592 | tf_op jit(solution)/shard_map/all_gather | solution.py:89
  305.9 62.9 %while.23 = (s32[]{:T(128)}, f32[32,128,256]{2,0,1:T(8,128)}, s32[4,32]{1,0:T(4,128)S(1)}, pred[4,32]{1,0:T(4,128)(4,1)S(1)}, bf16[4,32,128,128]{2,3,1,0:T(8,128...) while((s32[]{:T(128)}, f32[32,128,256]{2,0,1:T(8,128)}, ...), condition=%wide.region_4.5_spmd.clone, body=%wide.region_3.4_spmd.clone.sunk | while | flops 409998432 | bytes 40899864 | solution.py:53
  307.8 3.3 subtract_convert_fusion.5
  311.1 3.3 fusion.94
  314.4 6.2 fusion.95
  322.6 3.3 subtract_convert_fusion.5
  325.8 3.3 fusion.94
  329.2 7.5 fusion.95
  338.6 3.3 subtract_convert_fusion.5
  341.9 3.3 fusion.94
  345.2 7.5 fusion.95
  354.7 3.3 subtract_convert_fusion.5
  358.0 3.3 fusion.94
  361.3 7.5 fusion.95
  368.8 2.5 convert_element_type.50
  371.3 2.5 copy.24
  373.9 402.8 %all-reduce.2.cloned.1.call-done = f32[256,256]{1,0:T(8,128)} async-done(((f32[256,256]{1,0:T(8,128)}), f32[256,256]{1,0:T(8,128)}) %all-reduce.2.cloned.1.call-update) | async-done | bytes 262160 | tf_op jit(solution)/shard_map/psum | solution.py:90
  776.7 122.9 %reduce-scatter.5.cloned.1.call-done = bf16[128,256]{1,0:T(8,128)(2,1)} async-done(((bf16[4096,256]{1,0:T(8,128)(2,1)}), bf16[128,256]{1,0:T(8,128)(2,1)}) %reduce-scatter.5.cloned.1.call-update) | async-done | bytes 65552 | tf_op jit(solution)/shard_map/reduce_scatter | solution.py:100
  (79 shorter events, 29.1 us)
Async XLA Ops:
  7.2 212.2 %copy-start = (bf16[256,256]{1,0:T(8,128)(2,1)S(1)}, bf16[256,256]{1,0:T(8,128)(2,1)}, u32[]{:S(2)}) copy-start(bf16[256,256]{1,0:T(8,128)(2,1)} %param.12) | copy-start | bytes 393220
  7.2 88.0 %all-gather.3.cloned.1.call-start = ((), (), s32[]{:S(2)}) async-start(), calls=%async_computation.2 | async-start | bytes 2162688 | tf_op jit(solution)/shard_map/all_gather | solution.py:65
  7.9 211.4 %reduce-scatter.3.cloned.1.call-start = ((), (), s32[]{:S(2)}) async-start(), calls=%async_computation.3 | async-start | bytes 1114112 | tf_op jit(solution)/shard_map/reduce_scatter | solution.py:77
  141.5 77.8 %copy-start.3 = (bf16[128,256]{1,0:T(8,128)(2,1)S(1)}, bf16[128,256]{1,0:T(8,128)(2,1)}, u32[]{:S(2)}) copy-start(bf16[128,256]{1,0:T(8,128)(2,1)} %param.13) | copy-start | bytes 196612
  145.3 160.6 %all-gather.5.cloned.1.call-start = ((), (), s32[]{:S(2)}) async-start(), calls=%async_computation.4 | async-start | bytes 1114112 | tf_op jit(solution)/shard_map/all_gather | solution.py:89
  221.9 554.8 %all-reduce.2.cloned.1.call-start = ((), (), s32[]{:S(2)}) async-start(), calls=%async_computation.6 | async-start | bytes 524288 | tf_op jit(solution)/shard_map/psum | solution.py:90
  222.0 6.4 copy-start.2
  229.3 670.2 %reduce-scatter.5.cloned.1.call-start = ((), (), s32[]{:S(2)}) async-start(), calls=%async_computation.5 | async-start | bytes 2162688 | tf_op jit(solution)/shard_map/reduce_scatter | solution.py:100
  311.1 3.3 copy-start.1
  325.8 3.3 copy-start.1
  341.9 3.3 copy-start.1
  357.9 3.3 copy-start.1
Sparse Core Ops, SparseCore 0:
  11.1 83.9 all-gather.2
  145.4 73.9 reduce-scatter.2
  222.2 83.5 all-gather.4
  312.6 463.9 all-reduce.1
  781.5 117.9 reduce-scatter.4
where the time goes:
time: 909 us; the launch traced here: 908 us
  waiting for transfers between devices  760 us (84%)
  matrix products  95.6 us (11%)
  local copies, waits for them, and re-layouts  31.8 us (3%)
  between operations  14.5 us (2%)
    psum x1, waiting for transfers between devices, body(): grad_weight = lax.psum(weight_term, ('row', 'col'))  403 us
    reduce_scatter x1, waiting for transfers between devices, body(): lax.psum_scatter(back_terms.astype(jnp.bfloat16), 'row', scatter_dimensio...  123 us
    all_gather x1, waiting for transfers between devices, body(): whole_x = lax.all_gather(features, 'row', axis=0, tiled=True)  83.2 us
    all_gather x1, waiting for transfers between devices, body(): prop_grad = lax.all_gather(own_prop, 'col', axis=0, tiled=True)  76.5 us
    reduce_scatter x1, waiting for transfers between devices, body(): lax.psum_scatter(partial_value.astype(jnp.bfloat16), 'col', scatter_dimen...  74.1 us
    dot_general x8, matrix products, advance(): jnp.einsum('st,tif->sif', select, low, preferred_element_type=jnp.float32)  33.8 us
    dot_general x8, matrix products, advance(): jnp.einsum('st,tif->sif', select, high, preferred_element_type=jnp.float32)  32.3 us
    dot_general x8, matrix products, advance(): jnp.einsum(form, tile_block, picked, preferred_element_type=jnp.float32)  26 us
  transfers between devices with their start and end apart: 5, of which 5 were waited for; matrix products, arithmetic and copies ran while one was open for 9% of the time, Pallas kernels for 0%

commit v1 on v0

v1 whole, which is shorter than its diff:
```python
import functools

import jax
import jax.numpy as jnp
from jax import lax
from jax.experimental import pallas as pl
from jax.experimental.pallas import tpu as pltpu
from jax.sharding import PartitionSpec as P

MESH = pl.DeviceIdType.MESH
BF = jnp.bfloat16
F32 = jnp.float32
root_half = 0.7071067811865476
inv_root_tau = 0.3989422804014327
T = 128
H = 64
F = 256


class Place:
    def __init__(self):
        row, col = lax.axis_index("row"), lax.axis_index("col")
        self.zh, self.x, self.core = row // 8, (row // 2) % 4, row % 2
        self.zl, self.y = col // 4, col % 4

    def at(self, zh=None, x=None, core=None, zl=None, y=None):
        zh = self.zh if zh is None else zh % 4
        x = self.x if x is None else x % 4
        core = self.core if core is None else core
        zl = self.zl if zl is None else zl % 4
        y = self.y if y is None else y % 4
        return ((zh * 4 + x) * 2 + core, zl * 4 + y)


class Net:
    def __init__(self, send, recv):
        self.send, self.recv, self.started = send, recv, []

    def copy(self, src, dst, device):
        n = len(self.started)
        one = pltpu.make_async_remote_copy(
            src_ref=src,
            dst_ref=dst,
            send_sem=self.send.at[n],
            recv_sem=self.recv.at[n],
            device_id=device,
            device_id_type=MESH,
        )
        one.start()
        self.started.append(one)
        return one

    def drain(self):
        for one in self.started:
            one.wait_send()


def meet(partners):
    barrier = pltpu.get_barrier_semaphore()
    for device in partners:
        pl.semaphore_signal(barrier, inc=1, device_id=device, device_id_type=MESH)
    pl.semaphore_wait(barrier, len(partners))


class RingGather:
    def __init__(self, net, slot, p, dev):
        self.net, self.slot, self.p, self.dev = net, slot, p, dev

    def start(self):
        p, slot = self.p, self.slot
        self.up = self.net.copy(slot(p), slot(p), self.dev(p + 1))
        self.down = self.net.copy(slot(p), slot(p), self.dev(p - 1))

    def low(self):
        self.up.wait_recv()
        part = self.slot(self.p - 1).at[pl.ds(0, H)]
        self.up2 = self.net.copy(part, part, self.dev(self.p + 1))

    def high(self):
        self.down.wait_recv()
        part = self.slot(self.p + 1).at[pl.ds(H, H)]
        self.down2 = self.net.copy(part, part, self.dev(self.p - 1))

    def far(self):
        self.up2.wait_recv()
        self.down2.wait_recv()


class RingReduce:
    def __init__(self, net, src, land, pass_in, pass_out, p, dev):
        self.net, self.src, self.land, self.p, self.dev = net, src, land, p, dev
        self.pass_in, self.pass_out = pass_in, pass_out

    def start_far(self):
        p, src, net = self.p, self.src, self.net
        self.a = net.copy(src(p + 2, 0), self.pass_in.at[0], self.dev(p + 1))
        self.b = net.copy(src(p + 2, 1), self.pass_in.at[1], self.dev(p - 1))

    def start_near(self):
        p, src, net = self.p, self.src, self.net
        self.c1 = net.copy(src(p + 1, 1), self.land.at[0, 1], self.dev(p + 1))
        self.d0 = net.copy(src(p - 1, 0), self.land.at[1, 0], self.dev(p - 1))

    def mid(self):
        p, src, net = self.p, self.src, self.net
        self.a.wait_recv()
        total = src(p + 1, 0)[...].astype(F32) + self.pass_in[0].astype(F32)
        self.pass_out[0] = total.astype(BF)
        self.c0 = net.copy(self.pass_out.at[0], self.land.at[0, 0], self.dev(p + 1))
        self.b.wait_recv()
        total = src(p - 1, 1)[...].astype(F32) + self.pass_in[1].astype(F32)
        self.pass_out[1] = total.astype(BF)
        self.d1 = net.copy(self.pass_out.at[1], self.land.at[1, 1], self.dev(p - 1))

    def total(self, half):
        (self.c0 if half == 0 else self.c1).wait_recv()
        (self.d0 if half == 0 else self.d1).wait_recv()
        return (
            self.src(self.p, half)[...].astype(F32)
            + self.land[0, half].astype(F32)
            + self.land[1, half].astype(F32)
        )


def half_of(ref, half):
    return ref.at[pl.ds(half * H, H)]


def gather_x_kernel(own_ref, x_ref, send, recv):
    me = Place()
    net = Net(send, recv)
    sib = me.at(core=1 - me.core)
    meet([me.at(zh=me.zh + 1), me.at(zh=me.zh - 1), me.at(x=me.x + 1), me.at(x=me.x - 1), sib])
    x_ref[me.zh, me.x, me.core] = own_ref[...]

    def slot(zh, x):
        return x_ref.at[zh % 4, x % 4, me.core]

    across = []

    def swap(zh, x):
        across.append(net.copy(slot(zh, x), slot(zh, x), sib))

    rz = RingGather(net, lambda p: slot(p, me.x), me.zh, lambda p: me.at(zh=p))

    def ring_x(zh):
        ring = RingGather(net, lambda p: slot(zh, p), me.x, lambda p: me.at(x=p))
        ring.start()
        swap(zh, me.x)
        return ring

    def finish_x(ring, zh):
        ring.low()
        ring.high()
        swap(zh, me.x - 1)
        swap(zh, me.x + 1)

    def finish_far(ring, zh):
        ring.far()
        swap(zh, me.x + 2)

    rz.start()
    r0 = ring_x(me.zh)
    finish_x(r0, me.zh)
    finish_far(r0, me.zh)
    rz.low()
    r1 = ring_x(me.zh - 1)
    rz.high()
    r2 = ring_x(me.zh + 1)
    finish_x(r1, me.zh - 1)
    finish_x(r2, me.zh + 1)
    finish_far(r1, me.zh - 1)
    finish_far(r2, me.zh + 1)
    rz.far()
    r3 = ring_x(me.zh + 2)
    finish_x(r3, me.zh + 2)
    finish_far(r3, me.zh + 2)
    for one in across:
        one.wait_recv()
    net.drain()


def forward_kernel(place_ref, tiles_ref, x_ref, part_ref, tilebuf, dense, sem):
    load = pltpu.make_async_copy(tiles_ref, tilebuf.at[pl.ds(0, 128)], sem)
    load.start()
    tilebuf[128] = jnp.zeros((T, T), BF)
    load.wait()

    def build(r, _):
        for c in range(32):
            rows = pl.ds(pl.multiple_of(r * T, T), T)
            dense[c // 8, rows, pl.ds((c % 8) * T, T)] = tilebuf[place_ref[r * 32 + c]]
        return 0

    lax.fori_loop(0, 16, build, 0)

    def block(m, _):
        rows = pl.ds(pl.multiple_of(m * 512, 512), 512)
        total = jnp.zeros((512, F), F32)
        for zh in range(4):
            total += jnp.dot(dense[zh, rows], x_ref[zh], preferred_element_type=F32)
        part_ref[rows] = total.astype(BF)
        return 0

    lax.fori_loop(0, 4, block, 0)


def backward_kernel(place_ref, tiles_ref, g_ref, part_ref, tilebuf, dense, sem):
    load = pltpu.make_async_copy(tiles_ref, tilebuf.at[pl.ds(0, 128)], sem)
    load.start()
    tilebuf[128] = jnp.zeros((T, T), BF)
    load.wait()

    def turn(s, _):
        tilebuf[s] = tilebuf[s].T
        return 0

    lax.fori_loop(0, 128, turn, 0)

    def build(c, _):
        for r in range(16):
            rows = pl.ds(pl.multiple_of(c * T, T), T)
            dense[r // 4, rows, pl.ds((r % 4) * T, T)] = tilebuf[place_ref[r * 32 + c]]
        return 0

    lax.fori_loop(0, 32, build, 0)

    def block(m, _):
        rows = pl.ds(pl.multiple_of(m * 512, 512), 512)
        total = jnp.zeros((512, F), F32)
        for zl in range(4):
            total += jnp.dot(dense[zl, rows], g_ref[zl], preferred_element_type=F32)
        part_ref[rows] = total.astype(BF)
        return 0

    lax.fori_loop(0, 8, block, 0)


def layer_kernel(
    part_ref, w_ref, go_ref, hid_ref, g_ref, dw_ref, land, pass_in, pass_out, zsum, zland, send, recv
):
    me = Place()
    net = Net(send, recv)
    meet(
        [me.at(y=me.y + 1), me.at(y=me.y - 1), me.at(zl=me.zl + 1), me.at(zl=me.zl + 2), me.at(zl=me.zl + 3)]
    )
    rings = []
    for d in (1, 2, 3, 0):
        q = (me.zl + d) % 4

        def src(p, half, q=q):
            return half_of(part_ref.at[q, p % 4], half)

        rings.append(
            RingReduce(
                net, src, land.at[d], pass_in.at[d], pass_out.at[d], me.y, lambda p: me.at(y=p)
            )
        )
    for ring in rings:
        ring.start_far()
        ring.start_near()
    over = []
    for i, d in enumerate((1, 2, 3, 0)):
        rings[i].mid()
        if i:
            e = i - 1
            for half in range(2):
                zsum[e, pl.ds(half * H, H)] = rings[e].total(half).astype(BF)
            over.append(net.copy(zsum.at[e], zland.at[e], me.at(zl=me.zl + e + 1)))
    own = jnp.concatenate([rings[3].total(0), rings[3].total(1)], axis=0)
    for one in over:
        one.wait_recv()
    agg = (own + zland[0].astype(F32) + zland[1].astype(F32) + zland[2].astype(F32)).astype(BF)

    w = w_ref[...]
    pre = jnp.dot(agg, w, preferred_element_type=F32)
    erf = lax.erf(pre * root_half)
    slope = 0.5 * (1.0 + erf) + pre * jnp.exp(-0.5 * pre * pre) * inv_root_tau
    pre_grad = (go_ref[...].astype(F32) * slope).astype(BF)
    prop = lax.dot_general(pre_grad, w, (((1,), (1,)), ((), ())), preferred_element_type=F32)
    g_ref[me.zl, me.y] = prop.astype(BF)

    def slot(zl, y):
        return g_ref.at[zl % 4, y % 4]

    across = [
        net.copy(slot(me.zl, me.y), slot(me.zl, me.y), me.at(zl=me.zl + d)) for d in (1, 2, 3)
    ]

    def ring_y(zl):
        ring = RingGather(net, lambda p: slot(zl, p), me.y, lambda p: me.at(y=p))
        ring.start()
        return ring

    gathers = [ring_y(me.zl)]
    hid_ref[...] = (0.5 * pre * (1.0 + erf)).astype(BF)
    dw_ref[...] = lax.dot_general(agg, pre_grad, (((0,), (0,)), ((), ())), preferred_element_type=F32)
    for i, d in enumerate((1, 2, 3)):
        gathers[i].low()
        gathers[i].high()
        across[i].wait_recv()
        gathers.append(ring_y(me.zl - d))
    gathers[3].low()
    gathers[3].high()
    for ring in gathers:
        ring.far()
    net.drain()


def scatter_kernel(
    part_ref, dw_ref, gx_ref, gw_ref,
    cland, csum, land, pass_in, pass_out, zsum, zl_land, z_in, z_out,
    w1, w1in, w2, w2in, w3, w3in, w4in, w5in, w6, w7, send, recv,
):
    me = Place()
    net = Net(send, recv)
    sib = me.at(core=1 - me.core)
    meet(
        [sib]
        + [me.at(zh=me.zh + d) for d in (1, 2, 3)]
        + [me.at(x=me.x + d) for d in (1, 2, 3)]
        + [me.at(y=me.y + d) for d in (1, 2, 3)]
        + [me.at(zl=me.zl + d) for d in (1, 2, 3)]
    )
    order = (2, 1, 3, 0)
    swaps = []
    for i, d in enumerate(order):
        q = (me.zh + d) % 4
        swaps.append(net.copy(part_ref.at[q, :, 1 - me.core], cland.at[i], sib))
    a1 = net.copy(dw_ref.at[pl.ds(pl.multiple_of((1 - me.core) * T, T), T)], w1in, sib)

    rings = []
    for i, d in enumerate(order):
        q = (me.zh + d) % 4

        def src(p, half, i=i):
            return half_of(csum.at[i, p % 4], half)

        rings.append(
            RingReduce(net, src, land.at[i], pass_in.at[i], pass_out.at[i], me.x, lambda p: me.at(x=p))
        )

    def add_swap(i, d):
        q = (me.zh + d) % 4
        swaps[i].wait_recv()
        csum[i] = (part_ref[q, :, me.core].astype(F32) + cland[i].astype(F32)).astype(BF)
        rings[i].start_far()
        rings[i].start_near()

    def zsrc(p, half):
        return half_of(zsum.at[p % 4], half)

    zring = RingReduce(net, zsrc, zl_land, z_in, z_out, me.zh, lambda p: me.at(zh=p))

    def total_x(i, d):
        for half in range(2):
            zsum[(me.zh + d) % 4, pl.ds(half * H, H)] = rings[i].total(half).astype(BF)

    def w_core():
        a1.wait_recv()
        w1[...] = dw_ref[pl.ds(pl.multiple_of(me.core * T, T), T)] + w1in[...]

    def piece(ref, p, n):
        return ref.at[pl.ds(pl.multiple_of((p % 4) * n, n), n)]

    def w_spread(src, land_ref, p, dev, n):
        return [net.copy(piece(src, p + d, n), land_ref.at[d - 1], dev(p + d)) for d in (1, 2, 3)]

    def w_join(copies, src, land_ref, p, n, dst):
        for one in copies:
            one.wait_recv()
        dst[...] = piece(src, p, n)[...] + land_ref[0] + land_ref[1] + land_ref[2]

    def w_all(slots, p, dev):
        mine = slots.at[p]
        return [net.copy(mine, mine, dev(p + d)) for d in (1, 2, 3)]

    def w_sum(copies, slots):
        for one in copies:
            one.wait_recv()
        return slots[0] + slots[1] + slots[2] + slots[3]

    dev_x = lambda p: me.at(x=p)
    dev_y = lambda p: me.at(y=p)
    dev_zl = lambda p: me.at(zl=p)
    dev_zh = lambda p: me.at(zh=p)

    add_swap(0, order[0])
    add_swap(1, order[1])
    w_core()
    a2 = w_spread(w1, w2in, me.x, dev_x, 32)
    add_swap(2, order[2])
    add_swap(3, order[3])
    rings[0].mid()
    rings[1].mid()
    w_join(a2, w1, w2in, me.x, 32, w2)
    a3 = w_spread(w2, w3in, me.y, dev_y, 8)
    total_x(0, order[0])
    zring.start_far()
    rings[2].mid()
    w_join(a3, w2, w3in, me.y, 8, w3)
    w4in[me.zl] = w3[...]
    a4 = w_all(w4in, me.zl, dev_zl)
    total_x(1, order[1])
    rings[3].mid()
    total_x(2, order[2])
    zring.start_near()
    w5in[me.zh] = w_sum(a4, w4in)
    a5 = w_all(w5in, me.zh, dev_zh)
    total_x(3, order[3])
    w6[me.y] = w_sum(a5, w5in)
    a6 = w_all(w6, me.y, dev_y)
    zring.mid()
    for one in a6:
        one.wait_recv()
    w7[me.x] = w6[...]
    a7 = w_all(w7, me.x, dev_x)
    for one in a7:
        one.wait_recv()
    gw_ref[me.core] = w7[...].reshape(T, F)
    a8 = net.copy(gw_ref.at[me.core], gw_ref.at[me.core], sib)
    for half in range(2):
        gx_ref[pl.ds(half * H, H)] = zring.total(half).astype(BF)
    a8.wait_recv()
    net.drain()


VM = pl.BlockSpec(memory_space=pltpu.VMEM)
SM = pl.BlockSpec(memory_space=pltpu.SMEM)
ANY = pl.BlockSpec(memory_space=pl.ANY)
DMA = pltpu.SemaphoreType.DMA


def shape(*dims, dtype=BF):
    return jax.ShapeDtypeStruct(dims, dtype)


def params(collective_id=None):
    if collective_id is None:
        return pltpu.CompilerParams(vmem_limit_bytes=48 * 2**20)
    return pltpu.CompilerParams(
        collective_id=collective_id, has_side_effects=True, vmem_limit_bytes=48 * 2**20
    )


def body(features, weight, grad_out, tiles, tile_rows, tile_cols, tile_count):
    slots = jnp.arange(128, dtype=jnp.int32)
    spot = jnp.where(slots < tile_count[0, 0], tile_rows[0, 0] * 32 + tile_cols[0, 0], -1)
    spots = jnp.arange(512, dtype=jnp.int32)
    place = jnp.min(jnp.where(spot[None, :] == spots[:, None], slots[None, :], 128), axis=1)

    x = pl.pallas_call(
        gather_x_kernel,
        out_shape=shape(4, 4, 2, T, F),
        in_specs=[VM],
        out_specs=VM,
        scratch_shapes=[DMA((40,)), DMA((40,))],
        compiler_params=params(0),
    )(features)
    part = pl.pallas_call(
        forward_kernel,
        out_shape=shape(2048, F),
        in_specs=[SM, ANY, VM],
        out_specs=VM,
        scratch_shapes=[pltpu.VMEM((129, T, T), BF), pltpu.VMEM((4, 2048, 1024), BF), DMA],
        compiler_params=params(),
    )(place, tiles.reshape(128, T, T), x.reshape(4, 1024, F))
    hidden, g, dw = pl.pallas_call(
        layer_kernel,
        out_shape=[shape(T, F), shape(4, 4, T, F), shape(F, F, dtype=F32)],
        in_specs=[VM] * 3,
        out_specs=[VM] * 3,
        scratch_shapes=[
            pltpu.VMEM((4, 2, 2, H, F), BF),
            pltpu.VMEM((4, 2, H, F), BF),
            pltpu.VMEM((4, 2, H, F), BF),
            pltpu.VMEM((3, T, F), BF),
            pltpu.VMEM((3, T, F), BF),
            DMA((60,)),
            DMA((60,)),
        ],
        compiler_params=params(1),
    )(part.reshape(4, 4, T, F), weight, grad_out)
    back = pl.pallas_call(
        backward_kernel,
        out_shape=shape(4096, F),
        in_specs=[SM, ANY, VM],
        out_specs=VM,
        scratch_shapes=[pltpu.VMEM((129, T, T), BF), pltpu.VMEM((4, 4096, 512), BF), DMA],
        compiler_params=params(),
    )(place, tiles.reshape(128, T, T), g.reshape(4, 512, F))
    grad_features, grad_weight = pl.pallas_call(
        scatter_kernel,
        out_shape=[shape(T, F), shape(2, T, F, dtype=F32)],
        in_specs=[VM] * 2,
        out_specs=[VM] * 2,
        scratch_shapes=[
            pltpu.VMEM((4, 4, T, F), BF),
            pltpu.VMEM((4, 4, T, F), BF),
            pltpu.VMEM((4, 2, 2, H, F), BF),
            pltpu.VMEM((4, 2, H, F), BF),
            pltpu.VMEM((4, 2, H, F), BF),
            pltpu.VMEM((4, T, F), BF),
            pltpu.VMEM((2, 2, H, F), BF),
            pltpu.VMEM((2, H, F), BF),
            pltpu.VMEM((2, H, F), BF),
            pltpu.VMEM((T, F), F32),
            pltpu.VMEM((T, F), F32),
            pltpu.VMEM((32, F), F32),
            pltpu.VMEM((3, 32, F), F32),
            pltpu.VMEM((8, F), F32),
            pltpu.VMEM((3, 8, F), F32),
            pltpu.VMEM((4, 8, F), F32),
            pltpu.VMEM((4, 8, F), F32),
            pltpu.VMEM((4, 8, F), F32),
            pltpu.VMEM((4, 4, 8, F), F32),
            DMA((60,)),
            DMA((60,)),
        ],
        compiler_params=params(2),
    )(back.reshape(4, 4, 2, T, F), dw)
    return hidden, grad_features, grad_weight.reshape(F, F)


def solution(mesh):
    return jax.shard_map(
        body,
        mesh=mesh,
        in_specs=(
            P(("col", "row"), None),
            P(),
            P(("row", "col"), None),
            P("row", "col", None, None, None),
            P("row", "col", None),
            P("row", "col", None),
            P("row", "col"),
        ),
        out_specs=(P(("row", "col"), None), P(("col", "row"), None), P()),
        check_vma=False,
    )
```

time: 909 us -> 163 us (0.18)
  waiting for transfers between devices: 760 us -> 0 us
  Pallas kernels: 0 us -> 158 us
  matrix products: 95.6 us -> 0 us
  local copies, waits for them, and re-layouts: 31.8 us -> 2.81 us
  between operations: 14.5 us -> 1.36 us
    psum x1 -> x0, waiting for transfers between devices: 403 us -> none  [body(): grad_weight = lax.psum(weight_term, ('row', 'col'))]
    reduce_scatter x2 -> x0, waiting for transfers between devices: 197 us -> none  [the longest x1 123 us: body(): lax.psum_scatter(back_terms.astype(jnp.bfloat16), 'row', scatter_dimensio...]
    all_gather x2 -> x0, waiting for transfers between devices: 160 us -> none  [the longest x1 83.2 us: body(): whole_x = lax.all_gather(features, 'row', axis=0, tiled=True)]
    pallas_call x0 -> x5, Pallas kernels: none -> 158 us  [the longest x1 49.4 us: body(): pl.pallas_call(scatter_kernel, out_shape=[shape(T, F), shape(2, T, F, dty...]
    dot_general x27 -> x0, matrix products: 95.6 us -> none  [the longest x8 33.8 us: advance(): jnp.einsum('st,tif->sif', select, low, preferred_element_type=jnp.float32)]
    gather x8 -> x0, local copies, waits for them, and re-layouts: 16.7 us -> none  [advance(): picked = source[in_block]]
  transfers between devices with their start and end apart: 5 -> 0, of which waited for: 5 -> 0; matrix products, arithmetic and copies ran while one was open for 9% -> 0% of each run, Pallas kernels for 0% -> 0%
where the time goes in v1:
time: 163 us
  Pallas kernels  158 us (97%)
  local copies, waits for them, and re-layouts  2.81 us (2%)
    pallas_call x1, Pallas kernels, body(): pl.pallas_call(scatter_kernel, out_shape=[shape(T, F), shape(2, T, F, dty...  49.4 us
    pallas_call x1, Pallas kernels, body(): pl.pallas_call(gather_x_kernel, out_shape=shape(4, 4, 2, T, F), in_specs=...  38.3 us
    pallas_call x1, Pallas kernels, body(): pl.pallas_call(layer_kernel, out_shape=[shape(T, F), shape(4, 4, T, F), s...  37.2 us
    pallas_call x1, Pallas kernels, body(): pl.pallas_call(backward_kernel, out_shape=shape(4096, F), in_specs=[SM, A...  20.8 us
    pallas_call x1, Pallas kernels, body(): pl.pallas_call(forward_kernel, out_shape=shape(2048, F), in_specs=[SM, AN...  12.2 us

profile of v1, /device:TPU:1, one launch (start us, length us, event | category | flops | bytes accessed | tf_op | source)
XLA Modules:
  0.0 162.9 jit_solution(6477985037085879669)
XLA Ops:
  1.3 0.7 compare_select_fusion
  2.0 0.1 select_reduce_fusion.place_ref
  2.1 0.0 copy-start.1
  2.1 0.8 copy-done.1
  3.0 38.3 %shard_map.94 = bf16[4,4,2,128,256]{4,3,2,1,0:T(8,128)(2,1)S(1)} custom-call(bf16[128,256]{1,0:T(8,128)(2,1)S(1)} %copy-done.1), custom_call_target="tpu_custom_call" | custom-call | tf_op jit(solution)/shard_map/pallas_call | solution.py:452
  41.3 0.0 copy-start
  41.3 0.0 copy-start.2
  41.3 12.2 %shard_map.95 = bf16[2048,256]{1,0:T(8,128)(2,1)S(1)} custom-call(s32[512]{0:T(512)S(1)} %select_reduce_fusion.place_ref, bf16[128,128,128]{2,1,0:T(8,128)(2,1)} %bitcast.15, bf16[4,1024,256]{2,1,0:T(8,128)(2,1)S(1)} %bitcast.11), custom_call_target="tpu_custom_call" | custom-call | tf_op jit(solution)/shard_map/pallas_call | solution.py:460
  53.5 0.0 copy-done
  53.5 0.0 copy-done.2
  53.5 37.2 %shard_map.96 = (bf16[128,256]{1,0:T(8,128)(2,1)S(1)}, bf16[4,4,128,256]{3,2,1,0:T(8,128)(2,1)S(1)}, f32[256,256]{1,0:T(8,128)S(1)}) custom-call(bf16[4,4,128,256]{3,2,1,0:T(8,128)(2,1)S(1)} %bitcast.12, bf16[256,256]{1,0:T(8,128)(2,1)S(1)} %copy-done, bf16[128,256]{1,0:T(8,128)(2,1)S(1)} %copy-done.2), custom_call_target="tpu_custom_call" | custom-call | tf_op jit(solution)/shard_map/pallas_call | solution.py:468
  90.7 20.8 %shard_map.97 = bf16[4096,256]{1,0:T(8,128)(2,1)S(1)} custom-call(s32[512]{0:T(512)S(1)} %select_reduce_fusion.place_ref, bf16[128,128,128]{2,1,0:T(8,128)(2,1)} %bitcast.16, bf16[4,512,256]{2,1,0:T(8,128)(2,1)S(1)} %bitcast.13), custom_call_target="tpu_custom_call" | custom-call | tf_op jit(solution)/shard_map/pallas_call | solution.py:484
  111.6 49.4 %shard_map.98 = (bf16[128,256]{1,0:T(8,128)(2,1)S(1)}, f32[2,128,256]{2,1,0:T(8,128)S(1)}) custom-call(bf16[4,4,2,128,256]{4,3,2,1,0:T(8,128)(2,1)S(1)} %bitcast.10, f32[256,256]{1,0:T(8,128)S(1)} %get-tuple-element.10.dw_ref), custom_call_target="tpu_custom_call" | custom-call | tf_op jit(solution)/shard_map/pallas_call | solution.py:492
  160.9 0.6 copy.14
  161.6 0.6 copy.15
  162.2 0.7 copy.16
Async XLA Ops:
  2.1 0.8 copy-start.1
  41.3 12.2 %copy-start = (bf16[256,256]{1,0:T(8,128)(2,1)S(1)}, bf16[256,256]{1,0:T(8,128)(2,1)}, u32[]{:S(2)}) copy-start(bf16[256,256]{1,0:T(8,128)(2,1)} %w_ref.1) | copy-start | bytes 393220
  41.3 12.2 %copy-start.2 = (bf16[128,256]{1,0:T(8,128)(2,1)S(1)}, bf16[128,256]{1,0:T(8,128)(2,1)}, u32[]{:S(2)}) copy-start(bf16[128,256]{1,0:T(8,128)(2,1)} %go_ref.1) | copy-start | bytes 196612

commit v2 on v0

v2 whole, which is shorter than its diff:
```python
import jax
import jax.numpy as jnp
from jax import lax
from jax.experimental import pallas as pl
from jax.experimental.pallas import tpu as pltpu
from jax.sharding import PartitionSpec as P

MESH = pl.DeviceIdType.MESH
BF = jnp.bfloat16
F32 = jnp.float32
root_half = 0.7071067811865476
inv_root_tau = 0.3989422804014327
T = 128
F = 256


class Place:
    def __init__(self):
        row, col = lax.axis_index("row"), lax.axis_index("col")
        self.zh, self.x, self.core = row // 8, (row // 2) % 4, row % 2
        self.zl, self.y = col // 4, col % 4
        self.z = self.zh * 4 + self.zl

    def at(self, zh=None, x=None, core=None, zl=None, y=None):
        zh = self.zh if zh is None else zh % 4
        x = self.x if x is None else x % 4
        core = self.core if core is None else core
        zl = self.zl if zl is None else zl % 4
        y = self.y if y is None else y % 4
        return ((zh * 4 + x) * 2 + core, zl * 4 + y)

    def along_z(self, d):
        z = (self.z + d) % 16
        return self.at(zh=z // 4, zl=z % 4)


class Net:
    def __init__(self, send, recv):
        self.send, self.recv, self.started = send, recv, []

    def copy(self, src, dst, device):
        n = len(self.started)
        one = pltpu.make_async_remote_copy(
            src_ref=src,
            dst_ref=dst,
            send_sem=self.send.at[n],
            recv_sem=self.recv.at[n],
            device_id=device,
            device_id_type=MESH,
        )
        one.start()
        self.started.append(one)
        return one

    def drain(self):
        for one in self.started:
            one.wait_send()


def meet(partners):
    barrier = pltpu.get_barrier_semaphore()
    for device in partners:
        pl.semaphore_signal(barrier, inc=1, device_id=device, device_id_type=MESH)
    pl.semaphore_wait(barrier, len(partners))


def rows_of(i, n):
    return pl.ds(pl.multiple_of(i * n, n), n)


def layer_kernel(
    place_ref, features_ref, w_hbm, go_hbm, tiles_ref,
    hid_ref, gx_ref, gw_ref,
    tilebuf, dense, turned, x_ref, acc, part, yland, zsum, zland, w_ref, go_ref, g_ref, dw_ref,
    acc2, back, cland, csum, xland, hsum, hland, w1, w1in, w2in, w4, local, send, recv,
):
    me = Place()
    net = Net(send, recv)
    zh, x, core, zl, y = me.zh, me.x, me.core, me.zl, me.y
    sib = me.at(core=1 - core)
    cross = [(e // 4, e % 4) for e in range(1, 16)]

    def fetch(src, dst, n):
        one = pltpu.make_async_copy(src, dst, local.at[n])
        one.start()
        return one

    own_in = fetch(features_ref, x_ref.at[zh, x, core], 0)
    tiles_in = fetch(tiles_ref, tilebuf.at[pl.ds(0, 128)], 1)
    w_in = fetch(w_hbm, w_ref, 2)
    go_in = fetch(go_hbm, go_ref, 3)
    meet(
        [sib]
        + [me.along_z(d) for d in range(1, 16)]
        + [me.at(x=x + dx, y=y + dy) for dx, dy in cross]
    )
    own_in.wait()

    def slot(a, b):
        return x_ref.at[a % 4, b % 4, core]

    over_z, over_x, over_c = {}, {}, {}
    for d in (2, 1, 3):
        over_z[d] = net.copy(slot(zh, x), slot(zh, x), me.at(zh=zh + d))

    def send_c(d, e):
        over_c[d, e] = net.copy(slot(zh - d, x - e), slot(zh - d, x - e), sib)

    def send_x(d):
        for e in (2, 1, 3):
            over_x[d, e] = net.copy(slot(zh - d, x), slot(zh - d, x), me.at(x=x + e))
        send_c(d, 0)

    def land_x(d):
        for e in (1, 3, 2):
            over_x[d, e].wait_recv()
            send_c(d, e)

    def land_c(d):
        for e in range(4):
            over_c[d, e].wait_recv()

    send_x(0)
    tilebuf[128] = jnp.zeros((T, T), BF)
    tiles_in.wait()

    def build(r, _):
        for c in range(32):
            dense[c // 8, rows_of(r, T), pl.ds((c % 8) * T, T)] = tilebuf[place_ref[r * 32 + c]]
        return 0

    lax.fori_loop(0, 16, build, 0)
    land_x(0)

    def forward(d, first):
        a = (zh - d) % 4
        xs = x_ref.at[a].reshape(1024, F)

        def block(m, _):
            more = jnp.dot(dense[a, rows_of(m, 512)], xs[...], preferred_element_type=F32)
            if first:
                acc[rows_of(m, 512)] = more
            else:
                acc[rows_of(m, 512)] += more
            return 0

        lax.fori_loop(0, 4, block, 0)

    over_z[1].wait_recv()
    send_x(1)
    over_z[3].wait_recv()
    send_x(3)
    land_c(0)
    forward(0, True)
    land_x(1)
    land_x(3)
    over_z[2].wait_recv()
    send_x(2)
    land_c(1)
    forward(1, False)
    land_c(3)
    forward(3, False)
    land_x(2)
    land_c(2)

    far = (zh + 2) % 4
    last_x = x_ref.at[far].reshape(1024, F)
    over_y = {}
    for d in (1, 2, 3, 0):
        q = (zl + d) % 4
        more = jnp.dot(dense[far, rows_of(q, 512)], last_x[...], preferred_element_type=F32)
        part[q] = (acc[rows_of(q, 512)] + more).astype(BF).reshape(4, T, F)
        for e in (2, 1, 3):
            over_y[d, e] = net.copy(part.at[q, (y + e) % 4], yland.at[d, e - 1], me.at(y=y + e))

    def turn(s, _):
        tilebuf[s] = tilebuf[s].T
        return 0

    over_l = {}
    for i, d in enumerate((1, 2, 3, 0)):
        lax.fori_loop(i * 32, i * 32 + 32, turn, 0)
        total = part[(zl + d) % 4, y].astype(F32)
        for e in (1, 3, 2):
            over_y[d, e].wait_recv()
            total += yland[d, e - 1].astype(F32)
        if d:
            zsum[d - 1] = total.astype(BF)
            over_l[d] = net.copy(zsum.at[d - 1], zland.at[d - 1], me.at(zl=zl + d))

    def build_back(k):
        def step(c, _):
            for j in range(4):
                turned[k, rows_of(c, T), pl.ds(j * T, T)] = tilebuf[place_ref[(k * 4 + j) * 32 + c]]
            return 0

        lax.fori_loop(0, 32, step, 0)

    build_back(zl)
    w_in.wait()
    go_in.wait()
    for d in (1, 2, 3):
        over_l[d].wait_recv()
        total += zland[d - 1].astype(F32)
    agg = total.astype(BF)

    w = w_ref[...]
    pre = jnp.dot(agg, w, preferred_element_type=F32)
    erf = lax.erf(pre * root_half)
    slope = 0.5 * (1.0 + erf) + pre * jnp.exp(-0.5 * pre * pre) * inv_root_tau
    pre_grad = (go_ref[...].astype(F32) * slope).astype(BF)
    prop = lax.dot_general(pre_grad, w, (((1,), (1,)), ((), ())), preferred_element_type=F32)
    g_ref[zl, y] = prop.astype(BF)

    def gslot(a, b):
        return g_ref.at[a % 4, b % 4]

    back_l, back_y = {}, {}
    for d in (3, 2, 1):
        back_l[d] = net.copy(gslot(zl, y), gslot(zl, y), me.at(zl=zl + d))

    def send_y(d):
        for e in (2, 1, 3):
            back_y[d, e] = net.copy(gslot(zl - d, y), gslot(zl - d, y), me.at(y=y + e))

    def land_y(d):
        for e in (1, 3, 2):
            back_y[d, e].wait_recv()

    send_y(0)
    hid_ref[...] = (0.5 * pre * (1.0 + erf)).astype(BF)
    dw_ref[...] = lax.dot_general(agg, pre_grad, (((0,), (0,)), ((), ())), preferred_element_type=F32)
    w_core = net.copy(dw_ref.at[rows_of(1 - core, T)], w1in, sib)
    build_back((zl + 3) % 4)
    for d in (1, 3, 2):
        back_l[d].wait_recv()
        send_y(d)

    w_core.wait_recv()
    w1[...] = dw_ref[rows_of(core, T)] + w1in[...]

    def piece(ref, dx, dy):
        return ref.at[rows_of((x + dx) % 4 * 4 + (y + dy) % 4, 8)]

    w_cross = [
        net.copy(piece(w1, dx, dy), w2in.at[dx * 4 + dy - 1], me.at(x=x + dx, y=y + dy))
        for dx, dy in cross
    ]
    build_back((zl + 1) % 4)

    def backward(d, first):
        a = (zl - d) % 4
        gs = g_ref.at[a].reshape(512, F)

        def block(m, _):
            more = jnp.dot(turned[a, rows_of(m, 512)], gs[...], preferred_element_type=F32)
            if first:
                acc2[rows_of(m, 512)] = more
            else:
                acc2[rows_of(m, 512)] += more
            return 0

        lax.fori_loop(0, 8, block, 0)

    build_back((zl + 2) % 4)
    land_y(0)
    backward(0, True)
    land_y(1)
    backward(1, False)
    for one in w_cross:
        one.wait_recv()
    total = piece(w1, 0, 0)[...]
    for e in range(15):
        total += w2in[e]
    w4[me.z] = total
    w_z = [net.copy(w4.at[me.z], w4.at[me.z], me.along_z(d)) for d in range(1, 16)]
    land_y(3)
    backward(3, False)
    land_y(2)

    last = (zl + 2) % 4
    last_g = g_ref.at[last].reshape(512, F)
    order = (2, 1, 3, 0)
    swaps, back_x, back_z = {}, {}, {}
    for d in order:
        q = (zh + d) % 4
        for half in range(2):
            m = q * 2 + half
            more = jnp.dot(turned[last, rows_of(m, 512)], last_g[...], preferred_element_type=F32)
            back[q, pl.ds(half * 2, 2)] = (
                (acc2[rows_of(m, 512)] + more).astype(BF).reshape(2, 2, T, F)
            )
        swaps[d] = net.copy(back.at[q, :, 1 - core], cland.at[d], sib)
    for d in order:
        q = (zh + d) % 4
        swaps[d].wait_recv()
        csum[d] = (back[q, :, core].astype(F32) + cland[d].astype(F32)).astype(BF)
        for e in (2, 1, 3):
            back_x[d, e] = net.copy(csum.at[d, (x + e) % 4], xland.at[d, e - 1], me.at(x=x + e))

    def land_back(d):
        total = csum[d, x].astype(F32)
        for e in (1, 3, 2):
            back_x[d, e].wait_recv()
            total += xland[d, e - 1].astype(F32)
        if d:
            hsum[d - 1] = total.astype(BF)
            back_z[d] = net.copy(hsum.at[d - 1], hland.at[d - 1], me.at(zh=zh + d))
        return total

    land_back(2)
    land_back(1)
    land_back(3)
    total = land_back(0)
    for one in w_z:
        one.wait_recv()
    mine = gw_ref.at[core, rows_of(x * 4 + y, 8)]
    mine[...] = jnp.sum(w4[...], axis=0)
    w_back = [net.copy(mine, mine, me.at(x=x + dx, y=y + dy)) for dx, dy in cross]
    for d in (1, 3):
        back_z[d].wait_recv()
        total += hland[d - 1].astype(F32)
    for one in w_back:
        one.wait_recv()
    w_last = net.copy(gw_ref.at[core], gw_ref.at[core], sib)
    back_z[2].wait_recv()
    gx_ref[...] = (total + hland[1].astype(F32)).astype(BF)
    w_last.wait_recv()
    net.drain()


VM = pl.BlockSpec(memory_space=pltpu.VMEM)
SM = pl.BlockSpec(memory_space=pltpu.SMEM)
ANY = pl.BlockSpec(memory_space=pl.ANY)
DMA = pltpu.SemaphoreType.DMA


def shape(*dims, dtype=BF):
    return jax.ShapeDtypeStruct(dims, dtype)


def body(features, weight, grad_out, tiles, tile_rows, tile_cols, tile_count):
    slots = jnp.arange(128, dtype=jnp.int32)
    spot = jnp.where(slots < tile_count[0, 0], tile_rows[0, 0] * 32 + tile_cols[0, 0], -1)
    spots = jnp.arange(512, dtype=jnp.int32)
    place = jnp.min(jnp.where(spot[None, :] == spots[:, None], slots[None, :], 128), axis=1)
    b16 = lambda *dims: pltpu.VMEM(dims, BF)
    b32 = lambda *dims: pltpu.VMEM(dims, F32)
    hidden, grad_features, grad_weight = pl.pallas_call(
        layer_kernel,
        out_shape=[shape(T, F), shape(T, F), shape(2, T, F, dtype=F32)],
        in_specs=[SM, ANY, ANY, ANY, ANY],
        out_specs=[VM] * 3,
        scratch_shapes=[
            b16(129, T, T),
            b16(4, 2048, 1024),
            b16(4, 4096, 512),
            b16(4, 4, 2, T, F),
            b32(2048, F),
            b16(4, 4, T, F),
            b16(4, 3, T, F),
            b16(3, T, F),
            b16(3, T, F),
            b16(F, F),
            b16(T, F),
            b16(4, 4, T, F),
            b32(F, F),
            b32(4096, F),
            b16(4, 4, 2, T, F),
            b16(4, 4, T, F),
            b16(4, 4, T, F),
            b16(4, 3, T, F),
            b16(3, T, F),
            b16(3, T, F),
            b32(T, F),
            b32(T, F),
            b32(15, 8, F),
            b32(16, 8, F),
            DMA((4,)),
            DMA((144,)),
            DMA((144,)),
        ],
        compiler_params=pltpu.CompilerParams(
            collective_id=0, has_side_effects=True, vmem_limit_bytes=60 * 2**20
        ),
    )(place, features, weight, grad_out, tiles.reshape(128, T, T))
    return hidden, grad_features, grad_weight.reshape(F, F)


def solution(mesh):
    return jax.shard_map(
        body,
        mesh=mesh,
        in_specs=(
            P(("col", "row"), None),
            P(),
            P(("row", "col"), None),
            P("row", "col", None, None, None),
            P("row", "col", None),
            P("row", "col", None),
            P("row", "col"),
        ),
        out_specs=(P(("row", "col"), None), P(("col", "row"), None), P()),
        check_vma=False,
    )
```

time: 909 us -> 116 us (0.13)
  waiting for transfers between devices: 760 us -> 0 us
  Pallas kernels: 0 us -> 107 us
  matrix products: 95.6 us -> 0 us
  local copies, waits for them, and re-layouts: 31.8 us -> 4.61 us
  between operations: 14.5 us -> 1.29 us
    psum x1 -> x0, waiting for transfers between devices: 403 us -> none  [body(): grad_weight = lax.psum(weight_term, ('row', 'col'))]
    reduce_scatter x2 -> x0, waiting for transfers between devices: 197 us -> none  [the longest x1 123 us: body(): lax.psum_scatter(back_terms.astype(jnp.bfloat16), 'row', scatter_dimensio...]
    all_gather x2 -> x0, waiting for transfers between devices: 160 us -> none  [the longest x1 83.2 us: body(): whole_x = lax.all_gather(features, 'row', axis=0, tiled=True)]
    pallas_call x0 -> x1, Pallas kernels: none -> 107 us  [body(): pl.pallas_call(layer_kernel, out_shape=[shape(T, F), shape(T, F), shape(2...]
    dot_general x27 -> x0, matrix products: 95.6 us -> none  [the longest x8 33.8 us: advance(): jnp.einsum('st,tif->sif', select, low, preferred_element_type=jnp.float32)]
    gather x8 -> x0, local copies, waits for them, and re-layouts: 16.7 us -> none  [advance(): picked = source[in_block]]
  transfers between devices with their start and end apart: 5 -> 0, of which waited for: 5 -> 0; matrix products, arithmetic and copies ran while one was open for 9% -> 0% of each run, Pallas kernels for 0% -> 0%
where the time goes in v2:
time: 116 us; the launch traced here: 115 us
  Pallas kernels  107 us (92%)
  local copies, waits for them, and re-layouts  4.61 us (4%)
  other arithmetic  1.41 us (1%)
  between operations  1.29 us (1%)
    pallas_call x1, Pallas kernels, body(): pl.pallas_call(layer_kernel, out_shape=[shape(T, F), shape(T, F), shape(2...  107 us
    unnamed x3, local copies, waits for them, and re-layouts  4.61 us

profile of v2, /device:TPU:1, one launch (start us, length us, event | category | flops | bytes accessed | tf_op | source)
XLA Modules:
  0.0 114.7 jit_solution(11593786496985231076)
XLA Ops:
  1.3 0.7 compare_select_fusion
  2.0 0.7 select_reduce_fusion.place_ref
  2.7 107.4 %shard_map.94 = (bf16[128,256]{1,0:T(8,128)(2,1)}, bf16[128,256]{1,0:T(8,128)(2,1)}, f32[2,128,256]{2,1,0:T(8,128)}) custom-call(s32[512]{0:T(512)} %select_reduce_fusion.place_ref, bf16[128,256]{1,0:T(8,128)(2,1)} %features_ref.1, bf16[256,256]{1,0:T(8,128)(2,1)} %w_hbm.1, bf16[128,256]{1,0:T(8,128)(2,1)} %go_hbm.1, bf16[128,128,128]{2,1,0:T(8,128)(2,1)} %bitcast.6), custom_call_target="tpu_custom_call" | custom-call | tf_op jit(solution)/shard_map/pallas_call | solution.py:349
  110.1 1.5 %copy.14 = bf16[128,256]{1,0:T(8,128)(2,1)} copy(bf16[128,256]{1,0:T(8,128)(2,1)} %get-tuple-element.12) | data formatting | bytes 131072
  111.5 1.5 %copy.15 = bf16[128,256]{1,0:T(8,128)(2,1)} copy(bf16[128,256]{1,0:T(8,128)(2,1)} %get-tuple-element.13) | data formatting | bytes 131072
  113.0 1.7 %copy.16 = f32[256,256]{1,0:T(8,128)} copy(f32[256,256]{1,0:T(8,128)} %bitcast.7) | data formatting | bytes 524288

commit v3 on v2

--- a/solution.py
+++ b/solution.py
@@ -69,10 +69,11 @@
 
 
 def layer_kernel(
-    place_ref, features_ref, w_hbm, go_hbm, tiles_ref,
+    count_ref, rows_hbm, cols_hbm, features_ref, w_hbm, go_hbm, tiles_ref,
     hid_ref, gx_ref, gw_ref,
     tilebuf, dense, turned, x_ref, acc, part, yland, zsum, zland, w_ref, go_ref, g_ref, dw_ref,
-    acc2, back, cland, csum, xland, hsum, hland, w1, w1in, w2in, w4, local, send, recv,
+    acc2, back, cland, csum, xland, hsum, hland, w1, w1in, w2in, w4, spots, place_vm, place_ref,
+    local, send, recv,
 ):
     me = Place()
     net = Net(send, recv)
@@ -86,13 +87,16 @@
         return one
 
     own_in = fetch(features_ref, x_ref.at[zh, x, core], 0)
+    rows_in = fetch(rows_hbm, spots.at[0], 4)
+    cols_in = fetch(cols_hbm, spots.at[1], 5)
     tiles_in = fetch(tiles_ref, tilebuf.at[pl.ds(0, 128)], 1)
     w_in = fetch(w_hbm, w_ref, 2)
     go_in = fetch(go_hbm, go_ref, 3)
     meet(
-        [sib]
-        + [me.along_z(d) for d in range(1, 16)]
-        + [me.at(x=x + dx, y=y + dy) for dx, dy in cross]
+        [sib, me.at(zh=zh + 1), me.at(zh=zh - 1)]
+        + [me.at(x=x + d) for d in (1, 2, 3)]
+        + [me.at(y=y + d) for d in (1, 2, 3)]
+        + [me.at(zl=zl + d) for d in (1, 2, 3)]
     )
     own_in.wait()
 
@@ -100,8 +104,12 @@
         return x_ref.at[a % 4, b % 4, core]
 
     over_z, over_x, over_c = {}, {}, {}
-    for d in (2, 1, 3):
+    for d in (1, 3):
         over_z[d] = net.copy(slot(zh, x), slot(zh, x), me.at(zh=zh + d))
+
+    def pass_on(d, half):
+        part_of = slot(zh - d, x).at[pl.ds(half * 64, 64)]
+        over_z[d, half] = net.copy(part_of, part_of, me.at(zh=zh + d))
 
     def send_c(d, e):
         over_c[d, e] = net.copy(slot(zh - d, x - e), slot(zh - d, x - e), sib)
@@ -121,12 +129,24 @@
             over_c[d, e].wait_recv()
 
     send_x(0)
+
+    rows_in.wait()
+    cols_in.wait()
+    lane = lax.broadcasted_iota(jnp.int32, (T, T), 1)
+    slot_id = lax.broadcasted_iota(jnp.int32, (T, T), 0)
+    spot = jnp.where(lane < count_ref[0, 0], spots[0] * 32 + spots[1], -1)
+    spot = jnp.sum(jnp.where(lane == slot_id, spot, 0), axis=1, keepdims=True)
+    hit = spot == lax.broadcasted_iota(jnp.int32, (T, 512), 1)
+    found = jnp.where(hit, lax.broadcasted_iota(jnp.int32, (T, 512), 0) - 128, 0)
+    place_vm[...] = jnp.sum(found, axis=0, keepdims=True) + 128
+    place_in = fetch(place_vm, place_ref, 6)
     tilebuf[128] = jnp.zeros((T, T), BF)
     tiles_in.wait()
+    place_in.wait()
 
     def build(r, _):
         for c in range(32):
-            dense[c // 8, rows_of(r, T), pl.ds((c % 8) * T, T)] = tilebuf[place_ref[r * 32 + c]]
+            dense[c // 8, rows_of(r, T), pl.ds((c % 8) * T, T)] = tilebuf[place_ref[0, r * 32 + c]]
         return 0
 
     lax.fori_loop(0, 16, build, 0)
@@ -147,14 +167,17 @@
         lax.fori_loop(0, 4, block, 0)
 
     over_z[1].wait_recv()
+    pass_on(1, 0)
     send_x(1)
     over_z[3].wait_recv()
+    pass_on(3, 1)
     send_x(3)
     land_c(0)
     forward(0, True)
     land_x(1)
     land_x(3)
-    over_z[2].wait_recv()
+    over_z[1, 0].wait_recv()
+    over_z[3, 1].wait_recv()
     send_x(2)
     land_c(1)
     forward(1, False)
@@ -191,7 +214,7 @@
     def build_back(k):
         def step(c, _):
             for j in range(4):
-                turned[k, rows_of(c, T), pl.ds(j * T, T)] = tilebuf[place_ref[(k * 4 + j) * 32 + c]]
+                turned[k, rows_of(c, T), pl.ds(j * T, T)] = tilebuf[place_ref[0, (k * 4 + j) * 32 + c]]
             return 0
 
         lax.fori_loop(0, 32, step, 0)
@@ -309,20 +332,20 @@
         return total
 
     land_back(2)
-    land_back(1)
-    land_back(3)
-    total = land_back(0)
     for one in w_z:
         one.wait_recv()
     mine = gw_ref.at[core, rows_of(x * 4 + y, 8)]
     mine[...] = jnp.sum(w4[...], axis=0)
     w_back = [net.copy(mine, mine, me.at(x=x + dx, y=y + dy)) for dx, dy in cross]
+    land_back(1)
+    land_back(3)
+    total = land_back(0)
+    for one in w_back:
+        one.wait_recv()
+    w_last = net.copy(gw_ref.at[core], gw_ref.at[core], sib)
     for d in (1, 3):
         back_z[d].wait_recv()
         total += hland[d - 1].astype(F32)
-    for one in w_back:
-        one.wait_recv()
-    w_last = net.copy(gw_ref.at[core], gw_ref.at[core], sib)
     back_z[2].wait_recv()
     gx_ref[...] = (total + hland[1].astype(F32)).astype(BF)
     w_last.wait_recv()
@@ -339,17 +362,26 @@
     return jax.ShapeDtypeStruct(dims, dtype)
 
 
+def hand_over_kernel(a_ref, b_ref, c_ref, a_out, b_out, c_out, a_mid, b_mid, c_mid, sems):
+    triples = ((a_ref, a_mid, a_out), (b_ref, b_mid, b_out), (c_ref, c_mid, c_out))
+    inward = [pltpu.make_async_copy(src, mid, sems.at[0, n]) for n, (src, mid, _) in enumerate(triples)]
+    outward = [pltpu.make_async_copy(mid, dst, sems.at[1, n]) for n, (_, mid, dst) in enumerate(triples)]
+    for one in inward:
+        one.start()
+    for one, other in zip(inward, outward):
+        one.wait()
+        other.start()
+    for one in outward:
+        one.wait()
+
+
 def body(features, weight, grad_out, tiles, tile_rows, tile_cols, tile_count):
-    slots = jnp.arange(128, dtype=jnp.int32)
-    spot = jnp.where(slots < tile_count[0, 0], tile_rows[0, 0] * 32 + tile_cols[0, 0], -1)
-    spots = jnp.arange(512, dtype=jnp.int32)
-    place = jnp.min(jnp.where(spot[None, :] == spots[:, None], slots[None, :], 128), axis=1)
     b16 = lambda *dims: pltpu.VMEM(dims, BF)
     b32 = lambda *dims: pltpu.VMEM(dims, F32)
-    hidden, grad_features, grad_weight = pl.pallas_call(
+    found = pl.pallas_call(
         layer_kernel,
         out_shape=[shape(T, F), shape(T, F), shape(2, T, F, dtype=F32)],
-        in_specs=[SM, ANY, ANY, ANY, ANY],
+        in_specs=[SM] + [ANY] * 6,
         out_specs=[VM] * 3,
         scratch_shapes=[
             b16(129, T, T),
@@ -376,14 +408,32 @@
             b32(T, F),
             b32(15, 8, F),
             b32(16, 8, F),
-            DMA((4,)),
+            pltpu.VMEM((2, 1, T), jnp.int32),
+            pltpu.VMEM((1, 512), jnp.int32),
+            pltpu.SMEM((1, 512), jnp.int32),
+            DMA((8,)),
             DMA((144,)),
             DMA((144,)),
         ],
         compiler_params=pltpu.CompilerParams(
             collective_id=0, has_side_effects=True, vmem_limit_bytes=60 * 2**20
         ),
-    )(place, features, weight, grad_out, tiles.reshape(128, T, T))
+    )(
+        tile_count,
+        tile_rows.reshape(1, T),
+        tile_cols.reshape(1, T),
+        features,
+        weight,
+        grad_out,
+        tiles.reshape(128, T, T),
+    )
+    hidden, grad_features, grad_weight = pl.pallas_call(
+        hand_over_kernel,
+        out_shape=[shape(T, F), shape(T, F), shape(2, T, F, dtype=F32)],
+        in_specs=[ANY] * 3,
+        out_specs=[ANY] * 3,
+        scratch_shapes=[b16(T, F), b16(T, F), b32(2, T, F), DMA((2, 3))],
+    )(*found)
     return hidden, grad_features, grad_weight.reshape(F, F)
 
 

time: 116 us -> 103 us (0.89)
  Pallas kernels: 107 us -> 100 us
  local copies, waits for them, and re-layouts: 4.61 us -> 0 us
  other arithmetic: 1.41 us -> 0 us
    pallas_call x1, Pallas kernels: 107 us -> 98.4 us  [body(): pl.pallas_call(layer_kernel, out_shape=[shape(T, F), shape(T, F), shape(2...]
    unnamed x3 -> x0, local copies, waits for them, and re-layouts: 4.61 us -> none
    pallas_call x0 -> x1, Pallas kernels: none -> 1.78 us  [body(): pl.pallas_call(hand_over_kernel, out_shape=[shape(T, F), shape(T, F), sha...]
where the time goes in v3:
time: 103 us; the launch traced here: 101 us
  Pallas kernels  100 us (97%)
  between operations  1.29 us (1%)
    pallas_call x1, Pallas kernels, body(): pl.pallas_call(layer_kernel, out_shape=[shape(T, F), shape(T, F), shape(2...  98.4 us

profile of v3, /device:TPU:1, one launch (start us, length us, event | category | flops | bytes accessed | tf_op | source)
XLA Modules:
  0.0 101.5 jit_solution(7759683824940129772)
XLA Ops:
  1.3 98.4 %shard_map.94 = (bf16[128,256]{1,0:T(8,128)(2,1)}, bf16[128,256]{1,0:T(8,128)(2,1)}, f32[2,128,256]{2,1,0:T(8,128)}) custom-call(s32[1,1]{1,0:T(1,128)S(6)} %copy.10.count_ref, s32[1,128]{1,0:T(1,128)} %bitcast.5, s32[1,128]{1,0:T(1,128)} %bitcast.6, bf16[128,256]{1,0:T(8,128)(2,1)} %features_ref.1, bf16[256,256]{1,0:T(8,128)(2,1)} %w_hbm.1, ...), custom_call_target="tpu_custom_call" | custom-call | tf_op jit(solution)/shard_map/pallas_call | solution.py:381
  99.7 1.8 %shard_map.95 = (bf16[128,256]{1,0:T(8,128)(2,1)}, bf16[128,256]{1,0:T(8,128)(2,1)}, f32[2,128,256]{2,1,0:T(8,128)}) custom-call(bf16[128,256]{1,0:T(8,128)(2,1)} %get-tuple-element.9.a_ref, bf16[128,256]{1,0:T(8,128)(2,1)} %get-tuple-element.10.b_ref, f32[2,128,256]{2,1,0:T(8,128)} %get-tuple-element.11.c_ref), custom_call_target="tpu_custom_call" | custom-call | tf_op jit(solution)/shard_map/pallas_call | solution.py:430

commit v4 on v3

--- a/solution.py
+++ b/solution.py
@@ -69,10 +69,10 @@
 
 
 def layer_kernel(
-    count_ref, rows_hbm, cols_hbm, features_ref, w_hbm, go_hbm, tiles_ref,
+    count_hbm, rows_hbm, cols_hbm, features_ref, w_hbm, go_hbm, tiles_ref,
     hid_ref, gx_ref, gw_ref,
-    tilebuf, dense, turned, x_ref, acc, part, yland, zsum, zland, w_ref, go_ref, g_ref, dw_ref,
-    acc2, back, cland, csum, xland, hsum, hland, w1, w1in, w2in, w4, spots, place_vm, place_ref,
+    tilebuf, dense, turned, x_ref, acc, part, yland, zsum, zland, w_ref, wt_ref, go_ref, g_ref, dw_ref,
+    acc2, back, cland, csum, xland, hsum, hland, w1, w1in, w2in, w4, spots, place_vm, place_ref, count_ref,
     local, send, recv,
 ):
     me = Place()
@@ -87,6 +87,7 @@
         return one
 
     own_in = fetch(features_ref, x_ref.at[zh, x, core], 0)
+    count_in = fetch(count_hbm, count_ref, 7)
     rows_in = fetch(rows_hbm, spots.at[0], 4)
     cols_in = fetch(cols_hbm, spots.at[1], 5)
     tiles_in = fetch(tiles_ref, tilebuf.at[pl.ds(0, 128)], 1)
@@ -130,6 +131,7 @@
 
     send_x(0)
 
+    count_in.wait()
     rows_in.wait()
     cols_in.wait()
     lane = lax.broadcasted_iota(jnp.int32, (T, T), 1)
@@ -152,19 +154,34 @@
     lax.fori_loop(0, 16, build, 0)
     land_x(0)
 
+    def turn(s, _):
+        for j in range(8):
+            tilebuf[s * 8 + j] = tilebuf[s * 8 + j].T
+        return 0
+
+    def build_back(k):
+        def step(c, _):
+            for j in range(4):
+                turned[k, rows_of(c, T), pl.ds(j * T, T)] = tilebuf[place_ref[0, (k * 4 + j) * 32 + c]]
+            return 0
+
+        lax.fori_loop(0, 32, step, 0)
+
+    lax.fori_loop(0, 16, turn, 0)
+
     def forward(d, first):
         a = (zh - d) % 4
         xs = x_ref.at[a].reshape(1024, F)
 
         def block(m, _):
-            more = jnp.dot(dense[a, rows_of(m, 512)], xs[...], preferred_element_type=F32)
+            more = jnp.dot(dense[a, rows_of(m, 1024)], xs[...], preferred_element_type=F32)
             if first:
-                acc[rows_of(m, 512)] = more
+                acc[rows_of(m, 1024)] = more
             else:
-                acc[rows_of(m, 512)] += more
+                acc[rows_of(m, 1024)] += more
             return 0
 
-        lax.fori_loop(0, 4, block, 0)
+        lax.fori_loop(0, 2, block, 0)
 
     over_z[1].wait_recv()
     pass_on(1, 0)
@@ -174,6 +191,7 @@
     send_x(3)
     land_c(0)
     forward(0, True)
+    build_back((zl + 3) % 4)
     land_x(1)
     land_x(3)
     over_z[1, 0].wait_recv()
@@ -196,13 +214,10 @@
         for e in (2, 1, 3):
             over_y[d, e] = net.copy(part.at[q, (y + e) % 4], yland.at[d, e - 1], me.at(y=y + e))
 
-    def turn(s, _):
-        tilebuf[s] = tilebuf[s].T
-        return 0
-
     over_l = {}
-    for i, d in enumerate((1, 2, 3, 0)):
-        lax.fori_loop(i * 32, i * 32 + 32, turn, 0)
+    for d in (1, 2, 3, 0):
+        if d != 1:
+            build_back((zl + 4 - d) % 4)
         total = part[(zl + d) % 4, y].astype(F32)
         for e in (1, 3, 2):
             over_y[d, e].wait_recv()
@@ -211,16 +226,8 @@
             zsum[d - 1] = total.astype(BF)
             over_l[d] = net.copy(zsum.at[d - 1], zland.at[d - 1], me.at(zl=zl + d))
 
-    def build_back(k):
-        def step(c, _):
-            for j in range(4):
-                turned[k, rows_of(c, T), pl.ds(j * T, T)] = tilebuf[place_ref[0, (k * 4 + j) * 32 + c]]
-            return 0
-
-        lax.fori_loop(0, 32, step, 0)
-
-    build_back(zl)
     w_in.wait()
+    wt_ref[...] = w_ref[...].T
     go_in.wait()
     for d in (1, 2, 3):
         over_l[d].wait_recv()
@@ -232,7 +239,7 @@
     erf = lax.erf(pre * root_half)
     slope = 0.5 * (1.0 + erf) + pre * jnp.exp(-0.5 * pre * pre) * inv_root_tau
     pre_grad = (go_ref[...].astype(F32) * slope).astype(BF)
-    prop = lax.dot_general(pre_grad, w, (((1,), (1,)), ((), ())), preferred_element_type=F32)
+    prop = jnp.dot(pre_grad, wt_ref[...], preferred_element_type=F32)
     g_ref[zl, y] = prop.astype(BF)
 
     def gslot(a, b):
@@ -254,10 +261,6 @@
     hid_ref[...] = (0.5 * pre * (1.0 + erf)).astype(BF)
     dw_ref[...] = lax.dot_general(agg, pre_grad, (((0,), (0,)), ((), ())), preferred_element_type=F32)
     w_core = net.copy(dw_ref.at[rows_of(1 - core, T)], w1in, sib)
-    build_back((zl + 3) % 4)
-    for d in (1, 3, 2):
-        back_l[d].wait_recv()
-        send_y(d)
 
     w_core.wait_recv()
     w1[...] = dw_ref[rows_of(core, T)] + w1in[...]
@@ -269,27 +272,26 @@
         net.copy(piece(w1, dx, dy), w2in.at[dx * 4 + dy - 1], me.at(x=x + dx, y=y + dy))
         for dx, dy in cross
     ]
-    build_back((zl + 1) % 4)
+    for d in (1, 3, 2):
+        back_l[d].wait_recv()
+        send_y(d)
 
     def backward(d, first):
         a = (zl - d) % 4
         gs = g_ref.at[a].reshape(512, F)
 
         def block(m, _):
-            more = jnp.dot(turned[a, rows_of(m, 512)], gs[...], preferred_element_type=F32)
+            more = jnp.dot(turned[a, rows_of(m, 2048)], gs[...], preferred_element_type=F32)
             if first:
-                acc2[rows_of(m, 512)] = more
+                acc2[rows_of(m, 2048)] = more
             else:
-                acc2[rows_of(m, 512)] += more
+                acc2[rows_of(m, 2048)] += more
             return 0
 
-        lax.fori_loop(0, 8, block, 0)
-
-    build_back((zl + 2) % 4)
+        lax.fori_loop(0, 2, block, 0)
+
     land_y(0)
     backward(0, True)
-    land_y(1)
-    backward(1, False)
     for one in w_cross:
         one.wait_recv()
     total = piece(w1, 0, 0)[...]
@@ -297,6 +299,8 @@
         total += w2in[e]
     w4[me.z] = total
     w_z = [net.copy(w4.at[me.z], w4.at[me.z], me.along_z(d)) for d in range(1, 16)]
+    land_y(1)
+    backward(1, False)
     land_y(3)
     backward(3, False)
     land_y(2)
@@ -307,12 +311,8 @@
     swaps, back_x, back_z = {}, {}, {}
     for d in order:
         q = (zh + d) % 4
-        for half in range(2):
-            m = q * 2 + half
-            more = jnp.dot(turned[last, rows_of(m, 512)], last_g[...], preferred_element_type=F32)
-            back[q, pl.ds(half * 2, 2)] = (
-                (acc2[rows_of(m, 512)] + more).astype(BF).reshape(2, 2, T, F)
-            )
+        more = jnp.dot(turned[last, rows_of(q, 1024)], last_g[...], preferred_element_type=F32)
+        back[q] = (acc2[rows_of(q, 1024)] + more).astype(BF).reshape(4, 2, T, F)
         swaps[d] = net.copy(back.at[q, :, 1 - core], cland.at[d], sib)
     for d in order:
         q = (zh + d) % 4
@@ -332,13 +332,13 @@
         return total
 
     land_back(2)
+    land_back(1)
+    land_back(3)
     for one in w_z:
         one.wait_recv()
     mine = gw_ref.at[core, rows_of(x * 4 + y, 8)]
     mine[...] = jnp.sum(w4[...], axis=0)
     w_back = [net.copy(mine, mine, me.at(x=x + dx, y=y + dy)) for dx, dy in cross]
-    land_back(1)
-    land_back(3)
     total = land_back(0)
     for one in w_back:
         one.wait_recv()
@@ -353,7 +353,6 @@
 
 
 VM = pl.BlockSpec(memory_space=pltpu.VMEM)
-SM = pl.BlockSpec(memory_space=pltpu.SMEM)
 ANY = pl.BlockSpec(memory_space=pl.ANY)
 DMA = pltpu.SemaphoreType.DMA
 
@@ -381,7 +380,7 @@
     found = pl.pallas_call(
         layer_kernel,
         out_shape=[shape(T, F), shape(T, F), shape(2, T, F, dtype=F32)],
-        in_specs=[SM] + [ANY] * 6,
+        in_specs=[ANY] * 7,
         out_specs=[VM] * 3,
         scratch_shapes=[
             b16(129, T, T),
@@ -393,6 +392,7 @@
             b16(4, 3, T, F),
             b16(3, T, F),
             b16(3, T, F),
+            b16(F, F),
             b16(F, F),
             b16(T, F),
             b16(4, 4, T, F),
@@ -411,12 +411,13 @@
             pltpu.VMEM((2, 1, T), jnp.int32),
             pltpu.VMEM((1, 512), jnp.int32),
             pltpu.SMEM((1, 512), jnp.int32),
+            pltpu.SMEM((1, 1), jnp.int32),
             DMA((8,)),
             DMA((144,)),
             DMA((144,)),
         ],
         compiler_params=pltpu.CompilerParams(
-            collective_id=0, has_side_effects=True, vmem_limit_bytes=60 * 2**20
+            collective_id=0, has_side_effects=True, vmem_limit_bytes=57 * 2**20
         ),
     )(
         tile_count,

time: 103 us -> 96.6 us (0.938); the launches traced: 101 us -> 96.1 us
  Pallas kernels: 100 us -> 94.9 us
    pallas_call x1, Pallas kernels: 98.4 us -> 93.1 us  [body(): pl.pallas_call(layer_kernel, out_shape=[shape(T, F), shape(T, F), shape(2...]
where the time goes in v4:
time: 96.6 us; the launch traced here: 96.1 us
  Pallas kernels  94.9 us (98%)
  between operations  1.29 us (1%)
    pallas_call x1, Pallas kernels, body(): pl.pallas_call(layer_kernel, out_shape=[shape(T, F), shape(T, F), shape(2...  93.1 us

profile of v4, /device:TPU:1, one launch (start us, length us, event | category | flops | bytes accessed | tf_op | source)
XLA Modules:
  0.0 96.1 jit_solution(9337119366104230023)
XLA Ops:
  1.3 93.1 %shard_map.94 = (bf16[128,256]{1,0:T(8,128)(2,1)}, bf16[128,256]{1,0:T(8,128)(2,1)}, f32[2,128,256]{2,1,0:T(8,128)}) custom-call(s32[1,1]{1,0:T(1,128)S(6)} %copy.10.count_hbm, s32[1,128]{1,0:T(1,128)} %bitcast.5, s32[1,128]{1,0:T(1,128)} %bitcast.6, bf16[128,256]{1,0:T(8,128)(2,1)} %features_ref.1, bf16[256,256]{1,0:T(8,128)(2,1)} %w_hbm.1, ...), custom_call_target="tpu_custom_call" | custom-call | tf_op jit(solution)/shard_map/pallas_call | solution.py:380
  94.4 1.8 %shard_map.95 = (bf16[128,256]{1,0:T(8,128)(2,1)}, bf16[128,256]{1,0:T(8,128)(2,1)}, f32[2,128,256]{2,1,0:T(8,128)}) custom-call(bf16[128,256]{1,0:T(8,128)(2,1)} %get-tuple-element.9.a_ref, bf16[128,256]{1,0:T(8,128)(2,1)} %get-tuple-element.10.b_ref, f32[2,128,256]{2,1,0:T(8,128)} %get-tuple-element.11.c_ref), custom_call_target="tpu_custom_call" | custom-call | tf_op jit(solution)/shard_map/pallas_call | solution.py:431

commit v5 on v4

--- a/solution.py
+++ b/solution.py
@@ -38,13 +38,13 @@
     def __init__(self, send, recv):
         self.send, self.recv, self.started = send, recv, []
 
-    def copy(self, src, dst, device):
+    def copy(self, src, dst, device, recv=None):
         n = len(self.started)
         one = pltpu.make_async_remote_copy(
             src_ref=src,
             dst_ref=dst,
             send_sem=self.send.at[n],
-            recv_sem=self.recv.at[n],
+            recv_sem=self.recv.at[n] if recv is None else recv,
             device_id=device,
             device_id_type=MESH,
         )
@@ -52,6 +52,16 @@
         self.started.append(one)
         return one
 
+    def land(self, ref, recv, device):
+        pltpu.make_async_remote_copy(
+            src_ref=ref,
+            dst_ref=ref,
+            send_sem=self.send.at[0],
+            recv_sem=recv,
+            device_id=device,
+            device_id_type=MESH,
+        ).wait_recv()
+
     def drain(self):
         for one in self.started:
             one.wait_send()
@@ -73,13 +83,18 @@
     hid_ref, gx_ref, gw_ref,
     tilebuf, dense, turned, x_ref, acc, part, yland, zsum, zland, w_ref, wt_ref, go_ref, g_ref, dw_ref,
     acc2, back, cland, csum, xland, hsum, hland, w1, w1in, w2in, w4, spots, place_vm, place_ref, count_ref,
-    local, send, recv,
+    local, send, recv, recv_agg, recv_prop,
 ):
     me = Place()
     net = Net(send, recv)
     zh, x, core, zl, y = me.zh, me.x, me.core, me.zl, me.y
     sib = me.at(core=1 - core)
     cross = [(e // 4, e % 4) for e in range(1, 16)]
+
+    upper = zl // 2
+    inner = zl * (1 - upper) + (3 - zl) * upper
+    near = [s * (1 - upper) + (3 - s) * upper for s in (1 - inner, 2, 3)]
+    near.append(zl)
 
     def fetch(src, dst, n):
         one = pltpu.make_async_copy(src, dst, local.at[n])
@@ -207,31 +222,30 @@
     far = (zh + 2) % 4
     last_x = x_ref.at[far].reshape(1024, F)
     over_y = {}
-    for d in (1, 2, 3, 0):
-        q = (zl + d) % 4
+    for k in (2, 1, 0, 3):
+        q = near[k]
         more = jnp.dot(dense[far, rows_of(q, 512)], last_x[...], preferred_element_type=F32)
         part[q] = (acc[rows_of(q, 512)] + more).astype(BF).reshape(4, T, F)
         for e in (2, 1, 3):
-            over_y[d, e] = net.copy(part.at[q, (y + e) % 4], yland.at[d, e - 1], me.at(y=y + e))
-
-    over_l = {}
-    for d in (1, 2, 3, 0):
-        if d != 1:
-            build_back((zl + 4 - d) % 4)
-        total = part[(zl + d) % 4, y].astype(F32)
+            over_y[k, e] = net.copy(part.at[q, (y + e) % 4], yland.at[k, e - 1], me.at(y=y + e))
+
+    for i, k in enumerate((2, 1, 0, 3)):
+        if i:
+            build_back((zl + 3 - i) % 4)
+        total = part[near[k], y].astype(F32)
         for e in (1, 3, 2):
-            over_y[d, e].wait_recv()
-            total += yland[d, e - 1].astype(F32)
-        if d:
-            zsum[d - 1] = total.astype(BF)
-            over_l[d] = net.copy(zsum.at[d - 1], zland.at[d - 1], me.at(zl=zl + d))
+            over_y[k, e].wait_recv()
+            total += yland[k, e - 1].astype(F32)
+        if k < 3:
+            zsum[k] = total.astype(BF)
+            net.copy(zsum.at[k], zland.at[zl], me.at(zl=near[k]), recv_agg.at[zl])
 
     w_in.wait()
     wt_ref[...] = w_ref[...].T
     go_in.wait()
-    for d in (1, 2, 3):
-        over_l[d].wait_recv()
-        total += zland[d - 1].astype(F32)
+    for k in range(3):
+        net.land(zland.at[near[k]], recv_agg.at[near[k]], me.at(zl=near[k]))
+        total += zland[near[k]].astype(F32)
     agg = total.astype(BF)
 
     w = w_ref[...]
@@ -245,19 +259,19 @@
     def gslot(a, b):
         return g_ref.at[a % 4, b % 4]
 
-    back_l, back_y = {}, {}
-    for d in (3, 2, 1):
-        back_l[d] = net.copy(gslot(zl, y), gslot(zl, y), me.at(zl=zl + d))
-
-    def send_y(d):
+    back_y = {}
+    for k in (2, 1, 0):
+        net.copy(gslot(zl, y), gslot(zl, y), me.at(zl=near[k]), recv_prop.at[zl])
+
+    def send_y(k):
         for e in (2, 1, 3):
-            back_y[d, e] = net.copy(gslot(zl - d, y), gslot(zl - d, y), me.at(y=y + e))
-
-    def land_y(d):
+            back_y[k, e] = net.copy(gslot(near[k], y), gslot(near[k], y), me.at(y=y + e))
+
+    def land_y(k):
         for e in (1, 3, 2):
-            back_y[d, e].wait_recv()
-
-    send_y(0)
+            back_y[k, e].wait_recv()
+
+    send_y(3)
     hid_ref[...] = (0.5 * pre * (1.0 + erf)).astype(BF)
     dw_ref[...] = lax.dot_general(agg, pre_grad, (((0,), (0,)), ((), ())), preferred_element_type=F32)
     w_core = net.copy(dw_ref.at[rows_of(1 - core, T)], w1in, sib)
@@ -272,12 +286,12 @@
         net.copy(piece(w1, dx, dy), w2in.at[dx * 4 + dy - 1], me.at(x=x + dx, y=y + dy))
         for dx, dy in cross
     ]
-    for d in (1, 3, 2):
-        back_l[d].wait_recv()
-        send_y(d)
-
-    def backward(d, first):
-        a = (zl - d) % 4
+    for k in range(3):
+        net.land(gslot(near[k], y), recv_prop.at[near[k]], me.at(zl=near[k]))
+        send_y(k)
+
+    def backward(k, first):
+        a = near[k]
         gs = g_ref.at[a].reshape(512, F)
 
         def block(m, _):
@@ -290,8 +304,8 @@
 
         lax.fori_loop(0, 2, block, 0)
 
-    land_y(0)
-    backward(0, True)
+    land_y(3)
+    backward(3, True)
     for one in w_cross:
         one.wait_recv()
     total = piece(w1, 0, 0)[...]
@@ -299,13 +313,12 @@
         total += w2in[e]
     w4[me.z] = total
     w_z = [net.copy(w4.at[me.z], w4.at[me.z], me.along_z(d)) for d in range(1, 16)]
-    land_y(1)
-    backward(1, False)
-    land_y(3)
-    backward(3, False)
+    for k in range(2):
+        land_y(k)
+        backward(k, False)
     land_y(2)
 
-    last = (zl + 2) % 4
+    last = near[2]
     last_g = g_ref.at[last].reshape(512, F)
     order = (2, 1, 3, 0)
     swaps, back_x, back_z = {}, {}, {}
@@ -391,7 +404,7 @@
             b16(4, 4, T, F),
             b16(4, 3, T, F),
             b16(3, T, F),
-            b16(3, T, F),
+            b16(4, T, F),
             b16(F, F),
             b16(F, F),
             b16(T, F),
@@ -415,6 +428,8 @@
             DMA((8,)),
             DMA((144,)),
             DMA((144,)),
+            DMA((4,)),
+            DMA((4,)),
         ],
         compiler_params=pltpu.CompilerParams(
             collective_id=0, has_side_effects=True, vmem_limit_bytes=57 * 2**20

time: 96.6 us -> 95.8 us (level); the launches traced: 96.1 us -> 93.9 us
  Pallas kernels: 94.9 us -> 92.6 us
    pallas_call x1, Pallas kernels: 93.1 us -> 90.8 us  [body(): pl.pallas_call(layer_kernel, out_shape=[shape(T, F), shape(T, F), shape(2...]
where the time goes in v5:
time: 95.8 us; the launch traced here: 93.9 us
  Pallas kernels  92.6 us (97%)
  between operations  1.29 us (1%)
    pallas_call x1, Pallas kernels, body(): pl.pallas_call(layer_kernel, out_shape=[shape(T, F), shape(T, F), shape(2...  90.8 us

profile of v5, /device:TPU:1, one launch (start us, length us, event | category | flops | bytes accessed | tf_op | source)
XLA Modules:
  0.0 93.9 jit_solution(7066307378240012158)
XLA Ops:
  1.3 90.8 %shard_map.94 = (bf16[128,256]{1,0:T(8,128)(2,1)}, bf16[128,256]{1,0:T(8,128)(2,1)}, f32[2,128,256]{2,1,0:T(8,128)}) custom-call(s32[1,1]{1,0:T(1,128)S(6)} %copy.10.count_hbm, s32[1,128]{1,0:T(1,128)} %bitcast.5, s32[1,128]{1,0:T(1,128)} %bitcast.6, bf16[128,256]{1,0:T(8,128)(2,1)} %features_ref.1, bf16[256,256]{1,0:T(8,128)(2,1)} %w_hbm.1, ...), custom_call_target="tpu_custom_call" | custom-call | tf_op jit(solution)/shard_map/pallas_call | solution.py:393
  92.1 1.8 %shard_map.95 = (bf16[128,256]{1,0:T(8,128)(2,1)}, bf16[128,256]{1,0:T(8,128)(2,1)}, f32[2,128,256]{2,1,0:T(8,128)}) custom-call(bf16[128,256]{1,0:T(8,128)(2,1)} %get-tuple-element.9.a_ref, bf16[128,256]{1,0:T(8,128)(2,1)} %get-tuple-element.10.b_ref, f32[2,128,256]{2,1,0:T(8,128)} %get-tuple-element.11.c_ref), custom_call_target="tpu_custom_call" | custom-call | tf_op jit(solution)/shard_map/pallas_call | solution.py:446

commit v6 on v5

--- a/solution.py
+++ b/solution.py
@@ -272,7 +272,6 @@
             back_y[k, e].wait_recv()
 
     send_y(3)
-    hid_ref[...] = (0.5 * pre * (1.0 + erf)).astype(BF)
     dw_ref[...] = lax.dot_general(agg, pre_grad, (((0,), (0,)), ((), ())), preferred_element_type=F32)
     w_core = net.copy(dw_ref.at[rows_of(1 - core, T)], w1in, sib)
 
@@ -304,6 +303,7 @@
 
         lax.fori_loop(0, 2, block, 0)
 
+    hid_ref[...] = (0.5 * pre * (1.0 + erf)).astype(BF)
     land_y(3)
     backward(3, True)
     for one in w_cross:

time: 95.8 us -> 95.7 us (level)
  no operation moved by 1% of the time
where the time goes in v6:
time: 95.7 us; the launch traced here: 93.9 us
  Pallas kernels  92.6 us (97%)
  between operations  1.29 us (1%)
    pallas_call x1, Pallas kernels, body(): pl.pallas_call(layer_kernel, out_shape=[shape(T, F), shape(T, F), shape(2...  90.8 us

profile of v6, /device:TPU:1, one launch (start us, length us, event | category | flops | bytes accessed | tf_op | source)
XLA Modules:
  0.0 93.9 jit_solution(6297014004120117909)
XLA Ops:
  1.3 90.8 %shard_map.94 = (bf16[128,256]{1,0:T(8,128)(2,1)}, bf16[128,256]{1,0:T(8,128)(2,1)}, f32[2,128,256]{2,1,0:T(8,128)}) custom-call(s32[1,1]{1,0:T(1,128)S(6)} %copy.10.count_hbm, s32[1,128]{1,0:T(1,128)} %bitcast.5, s32[1,128]{1,0:T(1,128)} %bitcast.6, bf16[128,256]{1,0:T(8,128)(2,1)} %features_ref.1, bf16[256,256]{1,0:T(8,128)(2,1)} %w_hbm.1, ...), custom_call_target="tpu_custom_call" | custom-call | tf_op jit(solution)/shard_map/pallas_call | solution.py:393
  92.1 1.8 %shard_map.95 = (bf16[128,256]{1,0:T(8,128)(2,1)}, bf16[128,256]{1,0:T(8,128)(2,1)}, f32[2,128,256]{2,1,0:T(8,128)}) custom-call(bf16[128,256]{1,0:T(8,128)(2,1)} %get-tuple-element.9.a_ref, bf16[128,256]{1,0:T(8,128)(2,1)} %get-tuple-element.10.b_ref, f32[2,128,256]{2,1,0:T(8,128)} %get-tuple-element.11.c_ref), custom_call_target="tpu_custom_call" | custom-call | tf_op jit(solution)/shard_map/pallas_call | solution.py:446
